TPU v7x, 1024 devices: a whole 4x4x32 slice. The times are simulated.
1024 devices in a mesh: dp: 64 (over z, core), owner: 16 (over y, x).
Axes of the slice: x: 4, y: 4, z: 32, core: 2. Of those that a mesh axis runs over, the one named last changes fastest.
Arguments:
- activations: bfloat16 [8192, 4096], P('dp', 'owner'), may hold values from -6 to 6
- weight_tiles: bfloat16 [192, 8, 128, 128], P('owner'), may hold values from -0.1875 to 0.1875
- grad_out: bfloat16 [8192, 24576], P('dp', 'owner'), may hold values from -6 to 6
- tile_rows: int32 [112, 8], replicated, may hold values from 0 to 31, as said below
- col_owner: int32 [112], replicated, may hold values from 0 to 15, as said below
Outputs:
- output: bfloat16 [8192, 24576], P('dp', 'owner')
- grad_input: bfloat16 [8192, 4096], P('dp', 'owner')
- grad_weight: float32 [192, 131072], P('owner', 'dp')
Inputs may be any that keep to these rules, and one draw needn't show every extreme that they name: `col_owner`: each owner holds 1 to 12 tile columns and some owner holds exactly 12. The tiles and the output columns of an owner's columns fill its first slots in increasing column order; its other slots are unused. `tile_rows`: each tile column lists 8 distinct tile rows, in no particular order.
All inputs are finite; a program needn't handle non-finite values.
Results may differ from a plain program's by a relative error of at most 0.017.
Values may be sent and summed in bfloat16 or wider, within the bound.
A program may use at most 64 MiB of HBM per device.

v0:
```python
import math

import jax
import jax.numpy as jnp
from jax import lax
from jax.sharding import PartitionSpec as P


def slot_lists(col_owner, tile_rows, owner_idx, capacity):
    is_mine = (col_owner == owner_idx).astype(jnp.int32)
    col_rank = jnp.cumsum(is_mine) - 1
    slot_ids = jnp.arange(capacity, dtype=jnp.int32)
    chosen = ((col_rank[None, :] == slot_ids[:, None]) & (is_mine[None, :] == 1)).astype(jnp.int32)
    live_count = jnp.sum(chosen, axis=1)
    slot_rows = jnp.sum(chosen[:, :, None] * tile_rows[None, :, :], axis=1)
    return (slot_rows, live_count)


def weight_part(picked, grad_tiles, grad_scale, slot_count):
    tile_part = (
        jnp.einsum("tska,tsb->skab", picked, grad_tiles, preferred_element_type=jnp.float32)
        * grad_scale
    )
    return tile_part.reshape(slot_count, -1)


def weight_sums(picked, grad_tiles, grad_scale, capacity):
    return lax.psum_scatter(
        weight_part(picked, grad_tiles, grad_scale, capacity), "dp", scatter_dimension=1, tiled=True
    )


def input_grad(grad_tiles, weight_tiles, slot_rows, tok_rows, row_tiles):
    row_ids = jnp.arange(row_tiles, dtype=jnp.int32)
    grad_picked = jnp.einsum(
        "tsb,skab->tska", grad_tiles, weight_tiles, preferred_element_type=jnp.float32
    )
    onehot = (slot_rows.reshape(-1)[:, None] == row_ids[None, :]).astype(jnp.float32)
    dx_partial = jnp.einsum(
        "tja,jr->tra",
        grad_picked.reshape(tok_rows, -1, 128),
        onehot,
        precision=lax.Precision.HIGHEST,
    )
    dx_flat = dx_partial.reshape(tok_rows, row_tiles * 128)
    return lax.psum_scatter(dx_flat.astype(jnp.bfloat16), "owner", scatter_dimension=1, tiled=True)


def local(activations, weight_tiles, grad_out, tile_rows, col_owner):
    tok_rows = activations.shape[0]
    capacity = weight_tiles.shape[0]
    owner_idx = lax.axis_index("owner")
    full_input = lax.all_gather(activations, "owner", axis=1, tiled=True)
    row_tiles = full_input.shape[1] // 128
    input_tiles = full_input.reshape(tok_rows, row_tiles, 128)
    slot_rows, live_count = slot_lists(col_owner, tile_rows, owner_idx, capacity)
    picked = input_tiles[:, slot_rows, :]
    product = jnp.einsum("tska,skab->tsb", picked, weight_tiles, preferred_element_type=jnp.float32)
    live_f = live_count.astype(jnp.float32)[None, :, None]
    output = (product * live_f).astype(jnp.bfloat16).reshape(tok_rows, capacity * 128)
    live_mask = live_count.astype(jnp.bfloat16)[None, :, None]
    grad_tiles = grad_out.reshape(tok_rows, capacity, 128) * live_mask
    grad_scale = 1.0 / math.sqrt(tok_rows * lax.axis_size("dp"))
    grad_input = input_grad(grad_tiles, weight_tiles, slot_rows, tok_rows, row_tiles)
    grad_weight = weight_sums(picked, grad_tiles, grad_scale, capacity)
    return (output, grad_input, grad_weight)


def solution(mesh):
    in_specs = (P("dp", "owner"), P("owner", None, None, None), P("dp", "owner"), P(), P())
    out_specs = (P("dp", "owner"), P("dp", "owner"), P("owner", "dp"))
    return jax.shard_map(local, mesh=mesh, in_specs=in_specs, out_specs=out_specs, check_vma=False)
```

profile of v0, /device:TPU:6, one launch (start us, length us, event | category | flops | bytes accessed | tf_op | source)
XLA Modules:
  0.0 445.2 jit_solution(8614760228818816262)
XLA Ops:
  7.2 1.7 copy.44
  9.0 0.7 fusion.24
  9.7 0.7 copy.45
  10.4 1.2 copy.52
  11.6 1.6 reduce-window.8
  13.2 0.9 add_reduce_fusion
  14.2 1.0 multiply_reduce_fusion
  15.1 0.6 eq.52
  15.8 0.5 fusion.26
  16.4 1.5 fusion.12
  17.9 5.9 %fusion.6 = bf16[32,128,128]{2,0,1:T(8,128)(2,1)S(1)} fusion(f32[128,96,128]{2,0,1:T(8,128)S(1)} %bitcast.57, s32[96]{0:T(128)S(1)} %copy-done.3), kind=kOutput, calls=%fused_computation.6 | convolution fusion | flops 604507136 | bytes 7340416 | tf_op jit(solution)/shard_map/tja,jr->tra/dot_general | solution.py:39
  23.8 1.4 copy.75
  25.7 72.7 %all-gather.2.cloned.1.call-done = bf16[128,4096]{0,1:T(8,128)(2,1)} async-done(((bf16[128,256]{0,1:T(8,128)(2,1)}), bf16[128,4096]{0,1:T(8,128)(2,1)}) %all-gather.2.cloned.1.call-update) | async-done | bytes 1048592 | tf_op jit(solution)/shard_map/all_gather | solution.py:53
  98.4 2.3 copy.48
  100.7 4.0 gather_fusion
  104.7 4.6 %copy.49 = bf16[12,8,128,128]{2,3,1,0:T(8,128)(2,1)} copy(bf16[12,8,128,128]{3,2,1,0:T(8,128)(2,1)} %bitcast.54) | data formatting | bytes 6291456 | tf_op jit(solution)/shard_map/gather | solution.py:57
  109.4 2.9 broadcast_multiply_fusion
  112.3 0.7 pad.1
  113.0 8.1 %copy.69 = f32[2,8,1024,128]{3,1,2,0:T(8,128)} copy(f32[2,8,1024,128]{3,2,1,0:T(8,128)S(1)} %bitcast.53) | data formatting | bytes 16777216
  121.1 0.6 copy-done.4
  121.7 3.0 fusion.10
  124.7 0.9 copy.56
  125.6 87.2 %reduce-scatter.3.cloned.1.call-done = bf16[128,256]{1,0:T(8,128)(2,1)} async-done(((bf16[128,4096]{1,0:T(8,128)(2,1)}), bf16[128,256]{1,0:T(8,128)(2,1)}) %reduce-scatter.3.cloned.1.call-update) | async-done | bytes 65552 | tf_op jit(solution)/shard_map/reduce_scatter | solution.py:46
  212.9 225.8 %reduce-scatter.5.cloned.1.call-done = f32[12,2048]{1,0:T(8,128)} async-done(((f32[12,131072]{1,0:T(8,128)}), f32[12,2048]{1,0:T(8,128)}) %reduce-scatter.5.cloned.1.call-update) | async-done | bytes 98320 | tf_op jit(solution)/shard_map/reduce_scatter | solution.py:28
  (22 shorter events, 0.8 us)
Async XLA Ops:
  7.2 9.2 %copy-start = (bf16[12,8,128,128]{3,2,1,0:T(8,128)(2,1)S(1)}, bf16[12,8,128,128]{3,2,1,0:T(8,128)(2,1)}, u32[]{:S(2)}) copy-start(bf16[12,8,128,128]{3,2,1,0:T(8,128)(2,1)} %param.6) | copy-start | bytes 9437188
  7.2 91.2 %all-gather.2.cloned.1.call-start = ((), (), s32[]{:S(2)}) async-start(), calls=%async_computation.2 | async-start | bytes 1114112 | tf_op jit(solution)/shard_map/all_gather | solution.py:53
  9.0 203.9 %reduce-scatter.3.cloned.1.call-start = ((), (), s32[]{:S(2)}) async-start(), calls=%async_computation.3 | async-start | bytes 1114112 | tf_op jit(solution)/shard_map/reduce_scatter | solution.py:46
  16.4 1.5 copy-start.1
  16.4 1.5 copy-start.3
  25.2 413.4 %reduce-scatter.5.cloned.1.call-start = ((), (), s32[]{:S(2)}) async-start(), calls=%async_computation.4 | async-start | bytes 8519680 | tf_op jit(solution)/shard_map/reduce_scatter | solution.py:28
  104.7 4.6 %copy-start.2 = (bf16[12]{0:T(256)(128)(2,1)S(1)}, bf16[12]{0:T(256)(128)(2,1)}, u32[]{:S(2)}) copy-start(bf16[12]{0:T(256)(128)(2,1)} %copy-done.1) | copy-start | bytes 76
  121.1 0.7 copy-start.4
Sparse Core Ops, SparseCore 0:
  12.8 85.5 all-gather.1
  104.2 108.5 reduce-scatter.2
  217.2 221.3 reduce-scatter.4
where the time goes:
time: 447 us; the launch traced here: 445 us
  waiting for transfers between devices  386 us (86%)
  local copies, waits for them, and re-layouts  27.2 us (6%)
  between operations  13.8 us (3%)
  matrix products  13.3 us (3%)
  other arithmetic  4.78 us (1%)
    reduce_scatter x1, waiting for transfers between devices, weight_sums(): lax.psum_scatter(weight_part(picked, grad_tiles, grad_scale, capacity), '...  226 us
    reduce_scatter x1, waiting for transfers between devices, input_grad(): lax.psum_scatter(dx_flat.astype(jnp.bfloat16), 'owner', scatter_dimension...  87.2 us
    all_gather x1, waiting for transfers between devices, local(): full_input = lax.all_gather(activations, 'owner', axis=1, tiled=True)  72.7 us
    unnamed x16, local copies, waits for them, and re-layouts  14.7 us
  transfers between devices with their start and end apart: 3, of which 3 were waited for; matrix products, arithmetic and copies ran while one was open for 10% of the time, Pallas kernels for 0%

commit v1 on v0

v1 whole, which is shorter than its diff:
```python
import functools
import math

import jax
import jax.numpy as jnp
from jax import lax
from jax.experimental import pallas as pl
from jax.experimental.pallas import tpu as pltpu
from jax.sharding import PartitionSpec as P

MESH = pl.DeviceIdType.MESH
F32 = jnp.float32
BF16 = jnp.bfloat16
PIECES = 3


def kernel(
    dims,
    x_hbm, w_hbm, g_hbm, trt_ref, co_ref,
    out_ref, dx_ref, dw_ref,
    x_ref, xt, sib, xn, w, gcat, gt, dxs, dxr, part, ring_send, ring_recv, tbl, tbl_s,
    in_sem, tbl_sem, gsib_sem, ag_send, ag_recv, sib_send, sib_recv, dx_send, dx_recv, rs_send, rs_recv,
):
    ny, nx, nz, slots, per_col, scale = dims
    owners = ny * nx
    half = nz // 2
    group = slots // PIECES
    row_tiles = 2 * owners
    dp = lax.axis_index("dp")
    me = lax.axis_index("owner")
    z, core = dp // 2, dp % 2
    other = 1 - core
    y, x = me // nx, me % nx

    def dev(d, o):
        return {"dp": d, "owner": o}

    def peer_to(o):
        return ((y + o // nx) % ny) * nx + (x + o % nx) % nx

    def peer_from(o):
        return ((y + ny - o // nx) % ny) * nx + (x + nx - o % nx) % nx

    up = ((z + 1) % nz) * 2 + core
    down = ((z + nz - 1) % nz) * 2 + core
    sibling = z * 2 + other

    x_copy = pltpu.make_async_copy(x_hbm, x_ref, in_sem.at[0])
    g_load = pltpu.make_async_copy(g_hbm, gcat.at[0], in_sem.at[1])
    w_copy = pltpu.make_async_copy(w_hbm, w.at[:, pl.ds(0, per_col)], in_sem.at[2])
    x_copy.start()
    g_load.start()
    w_copy.start()
    g_ref = gcat.at[0]

    barrier = pltpu.get_barrier_semaphore()
    for o in range(1, owners):
        pl.semaphore_signal(barrier, inc=1, device_id=dev(dp, peer_to(o)), device_id_type=MESH)
    for d in (up, down, sibling):
        pl.semaphore_signal(barrier, inc=1, device_id=dev(d, me), device_id_type=MESH)

    x_copy.wait()
    for q in range(2):
        t = x_ref[:, q * 128:(q + 1) * 128].T
        for gi in range(4):
            for h in range(2):
                lo = gi * 32 + h * 16
                xt[2 * me + q, h, gi * 16:(gi + 1) * 16, :] = t[lo:lo + 16, :]
    pl.semaphore_wait(barrier, owners - 1 + 3)

    def ag_copy(o, tile):
        return pltpu.make_async_remote_copy(
            src_ref=xt.at[pl.ds(2 * tile, 2)],
            dst_ref=xt.at[pl.ds(2 * tile, 2)],
            send_sem=ag_send.at[o],
            recv_sem=ag_recv.at[o],
            device_id=dev(dp, peer_to(o)),
            device_id_type=MESH,
        )

    def sib_copy(o, tile):
        return pltpu.make_async_remote_copy(
            src_ref=xt.at[pl.ds(2 * tile, 2), other],
            dst_ref=sib.at[pl.ds(2 * tile, 2)],
            send_sem=sib_send.at[o],
            recv_sem=sib_recv.at[o],
            device_id=dev(sibling, me),
            device_id_type=MESH,
        )

    def dx_copy(o):
        return pltpu.make_async_remote_copy(
            src_ref=dxs.at[o],
            dst_ref=dxr.at[o],
            send_sem=dx_send.at[o],
            recv_sem=dx_recv.at[o],
            device_id=dev(dp, peer_to(o)),
            device_id_type=MESH,
        )

    def ring_copy(way, step, piece):
        return pltpu.make_async_remote_copy(
            src_ref=ring_send.at[way, step, pl.ds(piece * group, group)],
            dst_ref=ring_recv.at[way, step, pl.ds(piece * group, group)],
            send_sem=rs_send.at[way, step, piece],
            recv_sem=rs_recv.at[way, step, piece],
            device_id=dev(up if way == 0 else down, me),
            device_id_type=MESH,
        )

    g_copy = pltpu.make_async_remote_copy(
        src_ref=gcat.at[0],
        dst_ref=gcat.at[1],
        send_sem=gsib_sem.at[0],
        recv_sem=gsib_sem.at[1],
        device_id=dev(sibling, me),
        device_id_type=MESH,
    )

    @pl.loop(1, owners)
    def _(o):
        ag_copy(o, me).start()

    sib_copy(0, me).start()
    g_load.wait()
    g_copy.start()

    n_cols = co_ref.shape[1]
    mine = (co_ref[...] == me).astype(jnp.int32)
    sub = lax.broadcasted_iota(jnp.int32, (n_cols, n_cols), 0)
    lane = lax.broadcasted_iota(jnp.int32, (n_cols, n_cols), 1)
    mine_col = jnp.sum(jnp.where(sub == lane, mine, 0), axis=1, keepdims=True)
    rank = jnp.sum(jnp.where(sub < lane, mine_col, 0), axis=0, keepdims=True)
    slot_id = lax.broadcasted_iota(jnp.int32, (16, n_cols), 0)
    chosen = jnp.where((rank == slot_id) & (slot_id < slots), mine, 0)
    live_col = jnp.sum(chosen, axis=1, keepdims=True)
    tl = lax.broadcasted_iota(jnp.int32, (16, 128), 1)
    table = jnp.where(tl < row_tiles, per_col, 0)
    for k in range(per_col):
        row_col = jnp.sum(chosen * trt_ref[k:k + 1, :], axis=1, keepdims=True)
        found = (live_col == 1) & (tl < row_tiles) & (tl == row_col)
        table = jnp.where(found, k, jnp.where(tl == row_tiles + k, row_col, table))
    table = jnp.where(tl == row_tiles + per_col, live_col, table)
    tbl[...] = table
    tbl_copy = pltpu.make_async_copy(tbl, tbl_s, tbl_sem)
    tbl_copy.start()

    for s in range(slots):
        w[s, per_col] = jnp.zeros((128, 128), BF16)
        gt[s * 128:(s + 1) * 128, :] = g_ref[:, s * 128:(s + 1) * 128].T

    tbl_copy.wait()
    w_copy.wait()

    def dx_terms(o):
        owner = peer_to(o)
        for q in range(2):
            r = 2 * owner + q
            lhs = jnp.concatenate([w[s, tbl_s[s, r]] for s in range(slots)], axis=1)
            dxs[o, q] = jnp.dot(lhs, gt[...], preferred_element_type=F32).astype(BF16)

    @pl.loop(1, owners)
    def _(o):
        dx_terms(o)
        ag_copy(o, peer_from(o)).wait_recv()
        sib_copy(o, peer_from(o)).start()

    @pl.loop(1, owners)
    def _(o):
        dx_copy(o).start()

    @pl.loop(0, owners)
    def _(o):
        sib_copy(o, peer_from(o)).wait_recv()

    g_copy.wait_recv()

    def dw_terms(s):
        rows = [tbl_s[s, row_tiles + k] for k in range(per_col)]
        lhs = jnp.concatenate(
            [jnp.concatenate([xt[rk, core] for rk in rows], axis=0), jnp.concatenate([sib[rk] for rk in rows], axis=0)],
            axis=1,
        )
        lanes = pl.ds(pl.multiple_of(s * 128, 128), 128)
        rhs = jnp.concatenate([gcat[0, :, lanes], gcat[1, :, lanes]], axis=0)
        res = jnp.dot(lhs, rhs, preferred_element_type=F32)
        for c in range(4 * per_col):
            part[c, s] = res[c * 16:(c + 1) * 16, :]

    def dest(way, step):
        return (z + half - step) % nz if way == 0 else (z + nz - (half - 1 - step)) % nz

    def send_sum(way, step, piece, first):
        at = pl.ds(piece * group, group)
        total = part[dest(way, step), at]
        if not first:
            ring_copy(way, step - 1, piece).wait_recv()
            total = total + ring_recv[way, step - 1, at].astype(F32)
        ring_send[way, step, at] = total.astype(BF16)
        ring_copy(way, step, piece).start()

    for piece in range(PIECES):
        @pl.loop(piece * group, (piece + 1) * group)
        def _(s):
            dw_terms(s)
        for way in range(2):
            send_sum(way, 0, piece, True)

    turn_steps = 4
    turn_tiles = row_tiles // turn_steps

    def unit(u):
        @pl.when(u < turn_steps)
        def _():
            for j in range(turn_tiles):
                r = u * turn_tiles + j
                t = jnp.concatenate([xt[r, h, gi * 16:(gi + 1) * 16, :] for gi in range(4) for h in range(2)], axis=0)
                xn[r] = t.T

        @pl.when((u >= turn_steps) & (u < turn_steps + slots))
        def _():
            s = u - turn_steps
            lhs = jnp.concatenate([xn[tbl_s[s, row_tiles + k]] for k in range(per_col)], axis=1)
            rhs = jnp.concatenate([w[s, k] for k in range(per_col)], axis=0)
            live = tbl_s[s, row_tiles + per_col].astype(F32)
            out = jnp.dot(lhs, rhs, preferred_element_type=F32) * live
            out_ref[:, pl.ds(pl.multiple_of(s * 128, 128), 128)] = out.astype(BF16)

    @pl.loop(1, half - 1)
    def _(step):
        for piece in range(PIECES):
            for way in range(2):
                send_sum(way, step, piece, False)
        unit(step - 1)

    for piece in range(PIECES):
        send_sum(0, half - 1, piece, False)

    @pl.loop(half - 2, turn_steps + slots)
    def _(u):
        unit(u)

    dx_terms(0)

    def dx_add(o, total):
        dx_copy(o).wait_recv()
        return total + dxr[o].astype(F32)

    dx = lax.fori_loop(1, owners, dx_add, dxs[0].astype(F32))
    for q in range(2):
        dx_ref[:, q * 128:(q + 1) * 128] = dx[q].T.astype(BF16)

    for piece in range(PIECES):
        at = pl.ds(piece * group, group)
        ring_copy(1, half - 2, piece).wait_recv()
        total = part[z, at] + ring_recv[1, half - 2, at].astype(F32)
        ring_copy(0, half - 1, piece).wait_recv()
        total = total + ring_recv[0, half - 1, at].astype(F32)
        for i in range(group):
            s = piece * group + i
            live = tbl_s[s, row_tiles + per_col].astype(F32)
            dw_ref[s] = total[i] * (live * scale)

    @pl.loop(1, owners)
    def _(o):
        ag_copy(o, me).wait_send()
        dx_copy(o).wait_send()

    @pl.loop(0, owners)
    def _(o):
        sib_copy(o, me).wait_send()

    g_copy.wait_send()

    @pl.loop(0, half - 1)
    def _(step):
        for piece in range(PIECES):
            for way in range(2):
                ring_copy(way, step, piece).wait_send()

    for piece in range(PIECES):
        ring_copy(0, half - 1, piece).wait_send()


def local(ny, nx, n_dp, activations, weight_tiles, grad_out, tile_rows, col_owner):
    tokens, features = activations.shape
    slots, per_col = weight_tiles.shape[:2]
    owners = ny * nx
    nz = n_dp // 2
    half = nz // 2
    row_tiles = 2 * owners
    scale = 1.0 / math.sqrt(tokens * n_dp)
    vmem = pl.BlockSpec(memory_space=pltpu.VMEM)
    hbm = pl.BlockSpec(memory_space=pltpu.HBM)
    dma = pltpu.SemaphoreType.DMA
    out, dx, dw = pl.pallas_call(
        functools.partial(kernel, (ny, nx, nz, slots, per_col, scale)),
        out_shape=(
            jax.ShapeDtypeStruct(grad_out.shape, BF16),
            jax.ShapeDtypeStruct(activations.shape, BF16),
            jax.ShapeDtypeStruct((slots, 16, 128), F32),
        ),
        in_specs=[hbm, hbm, hbm, vmem, vmem],
        out_specs=(vmem, vmem, vmem),
        scratch_shapes=[
            pltpu.VMEM(activations.shape, BF16),
            pltpu.VMEM((row_tiles, 2, 64, tokens), BF16),
            pltpu.VMEM((row_tiles, 64, tokens), BF16),
            pltpu.VMEM((row_tiles, tokens, 128), BF16),
            pltpu.VMEM((slots, per_col + 1, 128, 128), BF16),
            pltpu.VMEM((2, tokens, slots * 128), BF16),
            pltpu.VMEM((slots * 128, tokens), BF16),
            pltpu.VMEM((owners, 2, 128, tokens), BF16),
            pltpu.VMEM((owners, 2, 128, tokens), BF16),
            pltpu.VMEM((nz, slots, 16, 128), F32),
            pltpu.VMEM((2, half, slots, 16, 128), BF16),
            pltpu.VMEM((2, half, slots, 16, 128), BF16),
            pltpu.VMEM((16, 128), jnp.int32),
            pltpu.SMEM((16, 128), jnp.int32),
            dma((3,)),
            dma(()),
            dma((2,)),
            dma((owners,)),
            dma((owners,)),
            dma((owners,)),
            dma((owners,)),
            dma((owners,)),
            dma((owners,)),
            dma((2, half, PIECES)),
            dma((2, half, PIECES)),
        ],
        compiler_params=pltpu.CompilerParams(
            collective_id=0, has_side_effects=True, vmem_limit_bytes=60 * 1024 * 1024
        ),
    )(activations, weight_tiles, grad_out, tile_rows.T, col_owner.reshape(1, -1))
    return out, dx, dw.reshape(slots, 2048)


def solution(mesh):
    owners, n_dp = mesh.shape["owner"], mesh.shape["dp"]
    nx = math.isqrt(owners)
    in_specs = (P("dp", "owner"), P("owner", None, None, None), P("dp", "owner"), P(), P())
    out_specs = (P("dp", "owner"), P("dp", "owner"), P("owner", "dp"))
    return jax.shard_map(
        functools.partial(local, owners // nx, nx, n_dp),
        mesh=mesh,
        in_specs=in_specs,
        out_specs=out_specs,
        check_vma=False,
    )
```

time: 447 us -> 99.8 us (0.22)
  the two profiles are of different devices: /device:TPU:6 before, /device:TPU:8 now
where the time goes in v1:
time: 99.8 us; the launch traced here: 99.5 us
  Pallas kernels  94 us (94%)
  local copies, waits for them, and re-layouts  4.84 us (5%)
    pallas_call x1, Pallas kernels, local(): pl.pallas_call(functools.partial(kernel, (ny, nx, nz, slots, per_col, sca...  94 us
    unnamed x4, local copies, waits for them, and re-layouts  4.84 us

profile of v1, /device:TPU:8, one launch (start us, length us, event | category | flops | bytes accessed | tf_op | source)
XLA Modules:
  0.0 99.5 jit_solution(4531720549832184402)
XLA Ops:
  0.6 94.0 %shard_map.76 = (bf16[128,1536]{1,0:T(8,128)(2,1)}, bf16[128,256]{1,0:T(8,128)(2,1)}, f32[12,16,128]{2,1,0:T(8,128)}) custom-call(bf16[128,256]{1,0:T(8,128)(2,1)} %x_hbm.1, bf16[12,8,128,128]{3,2,1,0:T(8,128)(2,1)} %w_hbm.1, bf16[128,1536]{1,0:T(8,128)(2,1)} %g_hbm.1, s32[8,112]{1,0:T(8,128)} %bitcast.7, s32[1,112]{1,0:T(1,128)} %bitcast.8), custom_call_target="tpu_custom_call" | custom-call | tf_op jit(solution)/shard_map/pallas_call | solution.py:296
  94.7 0.9 pad
  95.6 0.7 copy.8
  96.3 1.8 %copy.11 = bf16[128,1536]{1,0:T(8,128)(2,1)} copy(bf16[128,1536]{1,0:T(8,128)(2,1)} %get-tuple-element.12) | data formatting | bytes 786432
  98.0 1.5 %copy.12 = bf16[128,256]{1,0:T(8,128)(2,1)} copy(bf16[128,256]{1,0:T(8,128)(2,1)} %get-tuple-element.13) | data formatting | bytes 131072

commit v2 on v1

--- a/solution.py
+++ b/solution.py
@@ -12,18 +12,22 @@
 F32 = jnp.float32
 BF16 = jnp.bfloat16
 PIECES = 3
+NEAR = [(1, 1), (1, -1), (-1, 1), (-1, -1), (0, 1), (0, -1), (1, 0), (-1, 0)]
+FAR = [(0, 2), (1, 2), (-1, 2), (2, 0), (2, 1), (2, -1), (2, 2)]
 
 
 def kernel(
     dims,
     x_hbm, w_hbm, g_hbm, trt_ref, co_ref,
     out_ref, dx_ref, dw_ref,
-    x_ref, xt, sib, xn, w, gcat, gt, dxs, dxr, part, ring_send, ring_recv, tbl, tbl_s,
-    in_sem, tbl_sem, gsib_sem, ag_send, ag_recv, sib_send, sib_recv, dx_send, dx_recv, rs_send, rs_recv,
+    x_ref, xt, sib, xn, w, gcat, gt, dxs, dxr, part, pair_send, pair_recv, chain_send, chain_recv, tbl, tbl_s,
+    in_sem, tbl_sem, gsib_sem, ag_send, ag_recv, rl_send, rl_recv, sib_send, sib_recv, dx_send, dx_recv,
+    ps_send, ps_recv, cs_send, cs_recv,
 ):
     ny, nx, nz, slots, per_col, scale = dims
     owners = ny * nx
     half = nz // 2
+    steps = half // 2
     group = slots // PIECES
     row_tiles = 2 * owners
     dp = lax.axis_index("dp")
@@ -38,11 +42,12 @@
     def peer_to(o):
         return ((y + o // nx) % ny) * nx + (x + o % nx) % nx
 
-    def peer_from(o):
-        return ((y + ny - o // nx) % ny) * nx + (x + nx - o % nx) % nx
-
-    up = ((z + 1) % nz) * 2 + core
-    down = ((z + nz - 1) % nz) * 2 + core
+    def shift(v):
+        return ((y + ny + v[0]) % ny) * nx + (x + nx + v[1]) % nx
+
+    def along(way, links):
+        return dev(((z + links) % nz if way == 0 else (z + nz - links) % nz) * 2 + core, me)
+
     sibling = z * 2 + other
 
     x_copy = pltpu.make_async_copy(x_hbm, x_ref, in_sem.at[0])
@@ -56,8 +61,8 @@
     barrier = pltpu.get_barrier_semaphore()
     for o in range(1, owners):
         pl.semaphore_signal(barrier, inc=1, device_id=dev(dp, peer_to(o)), device_id_type=MESH)
-    for d in (up, down, sibling):
-        pl.semaphore_signal(barrier, inc=1, device_id=dev(d, me), device_id_type=MESH)
+    for d in (along(0, 1), along(1, 1), along(0, 2), along(1, 2), dev(sibling, me)):
+        pl.semaphore_signal(barrier, inc=1, device_id=d, device_id_type=MESH)
 
     x_copy.wait()
     for q in range(2):
@@ -66,24 +71,69 @@
             for h in range(2):
                 lo = gi * 32 + h * 16
                 xt[2 * me + q, h, gi * 16:(gi + 1) * 16, :] = t[lo:lo + 16, :]
-    pl.semaphore_wait(barrier, owners - 1 + 3)
-
-    def ag_copy(o, tile):
-        return pltpu.make_async_remote_copy(
-            src_ref=xt.at[pl.ds(2 * tile, 2)],
-            dst_ref=xt.at[pl.ds(2 * tile, 2)],
-            send_sem=ag_send.at[o],
-            recv_sem=ag_recv.at[o],
-            device_id=dev(dp, peer_to(o)),
-            device_id_type=MESH,
-        )
-
-    def sib_copy(o, tile):
+    pl.semaphore_wait(barrier, owners - 1 + 5)
+
+    def plane_copy(tile, at, n, send, recv, move):
+        here = pl.ds(2 * tile + at, n)
+        return pltpu.make_async_remote_copy(
+            src_ref=xt.at[here],
+            dst_ref=xt.at[here],
+            send_sem=send,
+            recv_sem=recv,
+            device_id=dev(dp, shift(move)),
+            device_id_type=MESH,
+        )
+
+    def quarter_copy(tile, q, h, send, recv, move):
+        return pltpu.make_async_remote_copy(
+            src_ref=xt.at[2 * tile + q, h],
+            dst_ref=xt.at[2 * tile + q, h],
+            send_sem=send,
+            recv_sem=recv,
+            device_id=dev(dp, shift(move)),
+            device_id_type=MESH,
+        )
+
+    def near_copy(v, tile):
+        i = NEAR.index(v)
+        return plane_copy(tile, 0, 2, ag_send.at[i], ag_recv.at[i], v)
+
+    def relay_copies(v, tile):
+        dy, dx = v
+        i = NEAR.index(v)
+        out = []
+        if dx:
+            q = 0 if dx > 0 else 1
+            out.append(plane_copy(tile, q, 1, rl_send.at[0, i], rl_recv.at[0, i], (0, dx)))
+        if dy:
+            q = 0 if dy > 0 else 1
+            out.append(plane_copy(tile, q, 1, rl_send.at[1, i], rl_recv.at[1, i], (dy, 0)))
+        if dx and dy:
+            q, h = 0 if dy > 0 else 1, 0 if dx > 0 else 1
+            out.append(quarter_copy(tile, q, h, rl_send.at[2, i], rl_recv.at[2, i], v))
+        return out
+
+    def relayed_copies(u, tile):
+        dy, dx = u
+        out = []
+        if dx == 2 and dy != 2:
+            for d in (1, -1):
+                out.append(relay_copies((dy, d), tile)[0])
+        elif dy == 2 and dx != 2:
+            for d in (1, -1):
+                out.append(relay_copies((d, dx), tile)[1 if dx else 0])
+        else:
+            for d in (1, -1):
+                for e in (1, -1):
+                    out.append(relay_copies((d, e), tile)[2])
+        return out
+
+    def sib_copy(i, tile):
         return pltpu.make_async_remote_copy(
             src_ref=xt.at[pl.ds(2 * tile, 2), other],
             dst_ref=sib.at[pl.ds(2 * tile, 2)],
-            send_sem=sib_send.at[o],
-            recv_sem=sib_recv.at[o],
+            send_sem=sib_send.at[i],
+            recv_sem=sib_recv.at[i],
             device_id=dev(sibling, me),
             device_id_type=MESH,
         )
@@ -98,13 +148,25 @@
             device_id_type=MESH,
         )
 
-    def ring_copy(way, step, piece):
-        return pltpu.make_async_remote_copy(
-            src_ref=ring_send.at[way, step, pl.ds(piece * group, group)],
-            dst_ref=ring_recv.at[way, step, pl.ds(piece * group, group)],
-            send_sem=rs_send.at[way, step, piece],
-            recv_sem=rs_recv.at[way, step, piece],
-            device_id=dev(up if way == 0 else down, me),
+    def pair_copy(way, step, piece):
+        at = pl.ds(piece * group, group)
+        return pltpu.make_async_remote_copy(
+            src_ref=pair_send.at[way, step, at],
+            dst_ref=pair_recv.at[way, step, at],
+            send_sem=ps_send.at[way, step, piece],
+            recv_sem=ps_recv.at[way, step, piece],
+            device_id=along(way, 1),
+            device_id_type=MESH,
+        )
+
+    def chain_copy(way, step, piece, links=2):
+        at = pl.ds(piece * group, group)
+        return pltpu.make_async_remote_copy(
+            src_ref=chain_send.at[way, step, at],
+            dst_ref=chain_recv.at[way, step, at],
+            send_sem=cs_send.at[way, step, piece],
+            recv_sem=cs_recv.at[way, step, piece],
+            device_id=along(way, links),
             device_id_type=MESH,
         )
 
@@ -117,9 +179,8 @@
         device_id_type=MESH,
     )
 
-    @pl.loop(1, owners)
-    def _(o):
-        ag_copy(o, me).start()
+    for v in NEAR:
+        near_copy(v, me).start()
 
     sib_copy(0, me).start()
     g_load.wait()
@@ -159,19 +220,36 @@
             lhs = jnp.concatenate([w[s, tbl_s[s, r]] for s in range(slots)], axis=1)
             dxs[o, q] = jnp.dot(lhs, gt[...], preferred_element_type=F32).astype(BF16)
 
-    @pl.loop(1, owners)
+    early = 1 + (owners - 1) * 2 // 5
+
+    @pl.loop(1, early)
     def _(o):
         dx_terms(o)
-        ag_copy(o, peer_from(o)).wait_recv()
-        sib_copy(o, peer_from(o)).start()
+
+    for i, v in enumerate(NEAR):
+        tile = shift((-v[0], -v[1]))
+        near_copy(v, tile).wait_recv()
+        for copy in relay_copies(v, tile):
+            copy.start()
+        sib_copy(1 + i, tile).start()
+
+    @pl.loop(early, owners)
+    def _(o):
+        dx_terms(o)
+
+    for i, u in enumerate(FAR):
+        tile = shift((-u[0], -u[1]))
+        for copy in relayed_copies(u, tile):
+            copy.wait_recv()
+        sib_copy(1 + len(NEAR) + i, tile).start()
 
     @pl.loop(1, owners)
     def _(o):
         dx_copy(o).start()
 
-    @pl.loop(0, owners)
-    def _(o):
-        sib_copy(o, peer_from(o)).wait_recv()
+    sib_copy(0, me).wait_recv()
+    for i, v in enumerate(NEAR + FAR):
+        sib_copy(1 + i, shift((-v[0], -v[1]))).wait_recv()
 
     g_copy.wait_recv()
 
@@ -187,24 +265,32 @@
         for c in range(4 * per_col):
             part[c, s] = res[c * 16:(c + 1) * 16, :]
 
-    def dest(way, step):
-        return (z + half - step) % nz if way == 0 else (z + nz - (half - 1 - step)) % nz
-
-    def send_sum(way, step, piece, first):
+    def dest(way, links):
+        return (z + links) % nz if way == 0 else (z + nz - links) % nz
+
+    def send_pair(way, step, piece):
         at = pl.ds(piece * group, group)
-        total = part[dest(way, step), at]
-        if not first:
-            ring_copy(way, step - 1, piece).wait_recv()
-            total = total + ring_recv[way, step - 1, at].astype(F32)
-        ring_send[way, step, at] = total.astype(BF16)
-        ring_copy(way, step, piece).start()
+        pair_send[way, step, at] = part[dest(way, half - 2 * step), at].astype(BF16)
+        pair_copy(way, step, piece).start()
+
+    def send_chain(way, step, piece, paired=True, chained=True, links=2):
+        at = pl.ds(piece * group, group)
+        total = part[dest(way, half - 1 - 2 * step), at]
+        if paired:
+            pair_copy(way, step, piece).wait_recv()
+            total = total + pair_recv[way, step, at].astype(F32)
+        if chained:
+            chain_copy(way, step - 1, piece).wait_recv()
+            total = total + chain_recv[way, step - 1, at].astype(F32)
+        chain_send[way, step, at] = total.astype(BF16)
+        chain_copy(way, step, piece, links).start()
 
     for piece in range(PIECES):
         @pl.loop(piece * group, (piece + 1) * group)
         def _(s):
             dw_terms(s)
-        for way in range(2):
-            send_sum(way, 0, piece, True)
+        send_pair(0, 0, piece)
+        send_chain(1, 0, piece, paired=False, chained=False, links=2 if steps > 1 else 1)
 
     turn_steps = 4
     turn_tiles = row_tiles // turn_steps
@@ -226,19 +312,33 @@
             out = jnp.dot(lhs, rhs, preferred_element_type=F32) * live
             out_ref[:, pl.ds(pl.multiple_of(s * 128, 128), 128)] = out.astype(BF16)
 
-    @pl.loop(1, half - 1)
+    per_step = (turn_steps + slots) // steps
+
+    def units(step):
+        for u in range(per_step):
+            unit(step * per_step + u)
+
+    for piece in range(PIECES):
+        send_chain(0, 0, piece, chained=False, links=2 if steps > 1 else 1)
+        if steps > 1:
+            send_pair(0, 1, piece)
+            send_pair(1, 1, piece)
+    units(0)
+
+    @pl.loop(1, steps - 1)
     def _(step):
         for piece in range(PIECES):
             for way in range(2):
-                send_sum(way, step, piece, False)
-        unit(step - 1)
-
-    for piece in range(PIECES):
-        send_sum(0, half - 1, piece, False)
-
-    @pl.loop(half - 2, turn_steps + slots)
-    def _(u):
-        unit(u)
+                send_chain(way, step, piece)
+            for way in range(2):
+                send_pair(way, step + 1, piece)
+        units(step)
+
+    if steps > 1:
+        for piece in range(PIECES):
+            for way in range(2):
+                send_chain(way, steps - 1, piece, links=1)
+        units(steps - 1)
 
     dx_terms(0)
 
@@ -250,36 +350,59 @@
     for q in range(2):
         dx_ref[:, q * 128:(q + 1) * 128] = dx[q].T.astype(BF16)
 
+    totals = []
     for piece in range(PIECES):
         at = pl.ds(piece * group, group)
-        ring_copy(1, half - 2, piece).wait_recv()
-        total = part[z, at] + ring_recv[1, half - 2, at].astype(F32)
-        ring_copy(0, half - 1, piece).wait_recv()
-        total = total + ring_recv[0, half - 1, at].astype(F32)
-        for i in range(group):
-            s = piece * group + i
-            live = tbl_s[s, row_tiles + per_col].astype(F32)
-            dw_ref[s] = total[i] * (live * scale)
+        total = part[z, at]
+        for way in range(2):
+            chain_copy(way, steps - 1, piece).wait_recv()
+            total = total + chain_recv[way, steps - 1, at].astype(F32)
+        totals += [total[i] * (tbl_s[piece * group + i, row_tiles + per_col].astype(F32) * scale) for i in range(group)]
+    total = jnp.stack(totals)
+    for i in range(16):
+        dw_ref[:, i * 128:(i + 1) * 128] = total[:, i, :]
 
     @pl.loop(1, owners)
     def _(o):
-        ag_copy(o, me).wait_send()
         dx_copy(o).wait_send()
 
+    for v in NEAR:
+        near_copy(v, me).wait_send()
+        for copy in relay_copies(v, me):
+            copy.wait_send()
+
     @pl.loop(0, owners)
-    def _(o):
-        sib_copy(o, me).wait_send()
+    def _(i):
+        sib_copy(i, me).wait_send()
 
     g_copy.wait_send()
 
-    @pl.loop(0, half - 1)
+    for way in range(2):
+        for piece in range(PIECES):
+            chain_copy(way, 0, piece).wait_send()
+            if way == 0:
+                pair_copy(way, 0, piece).wait_send()
+
+    @pl.loop(1, steps)
     def _(step):
         for piece in range(PIECES):
             for way in range(2):
-                ring_copy(way, step, piece).wait_send()
-
-    for piece in range(PIECES):
-        ring_copy(0, half - 1, piece).wait_send()
+                chain_copy(way, step, piece).wait_send()
+                pair_copy(way, step, piece).wait_send()
+
+
+def finish(a_ref, b_ref, c_ref, x_ref, y_ref, z_ref, a, b, c, load_sem, store_sem):
+    loads, stores = [], []
+    for i, (src, held, dst) in enumerate(((a_ref, a, x_ref), (b_ref, b, y_ref), (c_ref, c, z_ref))):
+        loads.append(pltpu.make_async_copy(src, held, load_sem.at[i]))
+        stores.append(pltpu.make_async_copy(held, dst, store_sem.at[i]))
+    for load in loads:
+        load.start()
+    for load, store in zip(loads, stores):
+        load.wait()
+        store.start()
+    for store in stores:
+        store.wait()
 
 
 def local(ny, nx, n_dp, activations, weight_tiles, grad_out, tile_rows, col_owner):
@@ -287,18 +410,18 @@
     slots, per_col = weight_tiles.shape[:2]
     owners = ny * nx
     nz = n_dp // 2
-    half = nz // 2
+    steps = nz // 4
     row_tiles = 2 * owners
     scale = 1.0 / math.sqrt(tokens * n_dp)
     vmem = pl.BlockSpec(memory_space=pltpu.VMEM)
     hbm = pl.BlockSpec(memory_space=pltpu.HBM)
     dma = pltpu.SemaphoreType.DMA
-    out, dx, dw = pl.pallas_call(
+    results = pl.pallas_call(
         functools.partial(kernel, (ny, nx, nz, slots, per_col, scale)),
         out_shape=(
             jax.ShapeDtypeStruct(grad_out.shape, BF16),
             jax.ShapeDtypeStruct(activations.shape, BF16),
-            jax.ShapeDtypeStruct((slots, 16, 128), F32),
+            jax.ShapeDtypeStruct((slots, 2048), F32),
         ),
         in_specs=[hbm, hbm, hbm, vmem, vmem],
         out_specs=(vmem, vmem, vmem),
@@ -313,27 +436,39 @@
             pltpu.VMEM((owners, 2, 128, tokens), BF16),
             pltpu.VMEM((owners, 2, 128, tokens), BF16),
             pltpu.VMEM((nz, slots, 16, 128), F32),
-            pltpu.VMEM((2, half, slots, 16, 128), BF16),
-            pltpu.VMEM((2, half, slots, 16, 128), BF16),
+            pltpu.VMEM((2, steps, slots, 16, 128), BF16),
+            pltpu.VMEM((2, steps, slots, 16, 128), BF16),
+            pltpu.VMEM((2, steps, slots, 16, 128), BF16),
+            pltpu.VMEM((2, steps, slots, 16, 128), BF16),
             pltpu.VMEM((16, 128), jnp.int32),
             pltpu.SMEM((16, 128), jnp.int32),
             dma((3,)),
             dma(()),
             dma((2,)),
+            dma((8,)),
+            dma((8,)),
+            dma((3, 8)),
+            dma((3, 8)),
             dma((owners,)),
             dma((owners,)),
             dma((owners,)),
             dma((owners,)),
-            dma((owners,)),
-            dma((owners,)),
-            dma((2, half, PIECES)),
-            dma((2, half, PIECES)),
+            dma((2, steps, PIECES)),
+            dma((2, steps, PIECES)),
+            dma((2, steps, PIECES)),
+            dma((2, steps, PIECES)),
         ],
         compiler_params=pltpu.CompilerParams(
             collective_id=0, has_side_effects=True, vmem_limit_bytes=60 * 1024 * 1024
         ),
     )(activations, weight_tiles, grad_out, tile_rows.T, col_owner.reshape(1, -1))
-    return out, dx, dw.reshape(slots, 2048)
+    return pl.pallas_call(
+        finish,
+        out_shape=tuple(jax.ShapeDtypeStruct(r.shape, r.dtype) for r in results),
+        in_specs=[hbm] * 3,
+        out_specs=(hbm,) * 3,
+        scratch_shapes=[pltpu.VMEM(r.shape, r.dtype) for r in results] + [dma((3,)), dma((3,))],
+    )(*results)
 
 
 def solution(mesh):

time: 99.8 us -> 75.9 us (0.76)
  the two profiles are of different devices: /device:TPU:8 before, /device:TPU:6 now
where the time goes in v2:
time: 75.9 us; the launch traced here: 75.3 us
  Pallas kernels  74.7 us (98%)
    pallas_call x1, Pallas kernels, local(): pl.pallas_call(functools.partial(kernel, (ny, nx, nz, slots, per_col, sca...  72.8 us
    pallas_call x1, Pallas kernels, local(): pl.pallas_call(finish, out_shape=tuple((jax.ShapeDtypeStruct(r.shape, r.d...  1.85 us

profile of v2, /device:TPU:6, one launch (start us, length us, event | category | flops | bytes accessed | tf_op | source)
XLA Modules:
  0.0 75.3 jit_solution(3953100377485473872)
XLA Ops:
  0.6 72.8 %shard_map.76 = (bf16[128,1536]{1,0:T(8,128)(2,1)}, bf16[128,256]{1,0:T(8,128)(2,1)}, f32[12,2048]{1,0:T(8,128)}) custom-call(bf16[128,256]{1,0:T(8,128)(2,1)} %x_hbm.1, bf16[12,8,128,128]{3,2,1,0:T(8,128)(2,1)} %w_hbm.1, bf16[128,1536]{1,0:T(8,128)(2,1)} %g_hbm.1, s32[8,112]{1,0:T(8,128)} %bitcast.2, s32[1,112]{1,0:T(1,128)} %bitcast.3), custom_call_target="tpu_custom_call" | custom-call | tf_op jit(solution)/shard_map/pallas_call | solution.py:419
  73.5 1.9 %shard_map.77 = (bf16[128,1536]{1,0:T(8,128)(2,1)}, bf16[128,256]{1,0:T(8,128)(2,1)}, f32[12,2048]{1,0:T(8,128)}) custom-call(bf16[128,1536]{1,0:T(8,128)(2,1)} %get-tuple-element.6.a_ref, bf16[128,256]{1,0:T(8,128)(2,1)} %get-tuple-element.7.b_ref, f32[12,2048]{1,0:T(8,128)} %get-tuple-element.8.c_ref), custom_call_target="tpu_custom_call" | custom-call | tf_op jit(solution)/shard_map/pallas_call | solution.py:465

commit v3 on v2

--- a/solution.py
+++ b/solution.py
@@ -159,14 +159,14 @@
             device_id_type=MESH,
         )
 
-    def chain_copy(way, step, piece, links=2):
+    def chain_copy(way, step, piece):
         at = pl.ds(piece * group, group)
         return pltpu.make_async_remote_copy(
             src_ref=chain_send.at[way, step, at],
             dst_ref=chain_recv.at[way, step, at],
             send_sem=cs_send.at[way, step, piece],
             recv_sem=cs_recv.at[way, step, piece],
-            device_id=along(way, links),
+            device_id=along(way, 2),
             device_id_type=MESH,
         )
 
@@ -243,54 +243,63 @@
             copy.wait_recv()
         sib_copy(1 + len(NEAR) + i, tile).start()
 
-    @pl.loop(1, owners)
-    def _(o):
-        dx_copy(o).start()
-
     sib_copy(0, me).wait_recv()
     for i, v in enumerate(NEAR + FAR):
         sib_copy(1 + i, shift((-v[0], -v[1]))).wait_recv()
 
     g_copy.wait_recv()
 
-    def dw_terms(s):
-        rows = [tbl_s[s, row_tiles + k] for k in range(per_col)]
-        lhs = jnp.concatenate(
-            [jnp.concatenate([xt[rk, core] for rk in rows], axis=0), jnp.concatenate([sib[rk] for rk in rows], axis=0)],
-            axis=1,
-        )
-        lanes = pl.ds(pl.multiple_of(s * 128, 128), 128)
-        rhs = jnp.concatenate([gcat[0, :, lanes], gcat[1, :, lanes]], axis=0)
-        res = jnp.dot(lhs, rhs, preferred_element_type=F32)
-        for c in range(4 * per_col):
-            part[c, s] = res[c * 16:(c + 1) * 16, :]
+    def dw_terms(ks):
+        @pl.loop(0, slots, unroll=4)
+        def _(s):
+            rows = [tbl_s[s, row_tiles + k] for k in ks]
+            lhs = jnp.concatenate(
+                [jnp.concatenate([xt[rk, core] for rk in rows], axis=0), jnp.concatenate([sib[rk] for rk in rows], axis=0)],
+                axis=1,
+            )
+            lanes = pl.ds(pl.multiple_of(s * 128, 128), 128)
+            rhs = jnp.concatenate([gcat[0, :, lanes], gcat[1, :, lanes]], axis=0)
+            res = jnp.dot(lhs, rhs, preferred_element_type=F32)
+            for j, k in enumerate(ks):
+                for gi in range(4):
+                    lo = j * 64 + gi * 16
+                    part[4 * k + gi, s] = res[lo:lo + 16, :]
+
+    first = ((z + half - 1) % nz) // 4
+    dw_rounds = (per_col - 2) // 2
+
+    def dw_round(step):
+        dw_terms([(first + 2 * per_col - 1 - step) % per_col, (first + 2 + step) % per_col])
 
     def dest(way, links):
         return (z + links) % nz if way == 0 else (z + nz - links) % nz
 
     def send_pair(way, step, piece):
         at = pl.ds(piece * group, group)
-        pair_send[way, step, at] = part[dest(way, half - 2 * step), at].astype(BF16)
+        pair_send[way, step, at] = part[dest(way, half - 1 - 2 * step), at].astype(BF16)
         pair_copy(way, step, piece).start()
 
-    def send_chain(way, step, piece, paired=True, chained=True, links=2):
+    def send_chain(way, step, piece, paired=True, chained=True):
         at = pl.ds(piece * group, group)
-        total = part[dest(way, half - 1 - 2 * step), at]
+        total = part[dest(way, half - 2 * step), at]
         if paired:
-            pair_copy(way, step, piece).wait_recv()
-            total = total + pair_recv[way, step, at].astype(F32)
+            pair_copy(way, step - 1, piece).wait_recv()
+            total = total + pair_recv[way, step - 1, at].astype(F32)
         if chained:
             chain_copy(way, step - 1, piece).wait_recv()
             total = total + chain_recv[way, step - 1, at].astype(F32)
         chain_send[way, step, at] = total.astype(BF16)
-        chain_copy(way, step, piece, links).start()
-
+        chain_copy(way, step, piece).start()
+
+    dw_terms([first, (first + 1) % per_col] if per_col > 1 else [first])
     for piece in range(PIECES):
-        @pl.loop(piece * group, (piece + 1) * group)
-        def _(s):
-            dw_terms(s)
-        send_pair(0, 0, piece)
-        send_chain(1, 0, piece, paired=False, chained=False, links=2 if steps > 1 else 1)
+        send_chain(0, 0, piece, paired=False, chained=False)
+        for way in range(2):
+            send_pair(way, 0, piece)
+
+    @pl.loop(1, owners)
+    def _(o):
+        dx_copy(o).start()
 
     turn_steps = 4
     turn_tiles = row_tiles // turn_steps
@@ -318,27 +327,33 @@
         for u in range(per_step):
             unit(step * per_step + u)
 
-    for piece in range(PIECES):
-        send_chain(0, 0, piece, chained=False, links=2 if steps > 1 else 1)
-        if steps > 1:
-            send_pair(0, 1, piece)
-            send_pair(1, 1, piece)
+    if dw_rounds > 0:
+        dw_round(0)
     units(0)
 
-    @pl.loop(1, steps - 1)
+    if steps > 1:
+        for piece in range(PIECES):
+            send_chain(0, 1, piece)
+            send_chain(1, 1, piece, chained=False)
+            for way in range(2):
+                send_pair(way, 1, piece)
+        if dw_rounds > 1:
+            dw_round(1)
+        units(1)
+
+    @pl.loop(2, steps)
     def _(step):
         for piece in range(PIECES):
             for way in range(2):
                 send_chain(way, step, piece)
             for way in range(2):
-                send_pair(way, step + 1, piece)
+                send_pair(way, step, piece)
+
+        @pl.when(step < dw_rounds)
+        def _():
+            dw_round(step)
+
         units(step)
-
-    if steps > 1:
-        for piece in range(PIECES):
-            for way in range(2):
-                send_chain(way, steps - 1, piece, links=1)
-        units(steps - 1)
 
     dx_terms(0)
 
@@ -355,8 +370,11 @@
         at = pl.ds(piece * group, group)
         total = part[z, at]
         for way in range(2):
-            chain_copy(way, steps - 1, piece).wait_recv()
-            total = total + chain_recv[way, steps - 1, at].astype(F32)
+            pair_copy(way, steps - 1, piece).wait_recv()
+            total = total + pair_recv[way, steps - 1, at].astype(F32)
+            if way == 0 or steps > 1:
+                chain_copy(way, steps - 1, piece).wait_recv()
+                total = total + chain_recv[way, steps - 1, at].astype(F32)
         totals += [total[i] * (tbl_s[piece * group + i, row_tiles + per_col].astype(F32) * scale) for i in range(group)]
     total = jnp.stack(totals)
     for i in range(16):
@@ -379,9 +397,9 @@
 
     for way in range(2):
         for piece in range(PIECES):
-            chain_copy(way, 0, piece).wait_send()
+            pair_copy(way, 0, piece).wait_send()
             if way == 0:
-                pair_copy(way, 0, piece).wait_send()
+                chain_copy(way, 0, piece).wait_send()
 
     @pl.loop(1, steps)
     def _(step):

time: 75.9 us -> 73.2 us (0.964)
  Pallas kernels: 74.7 us -> 71.9 us
    pallas_call x1, Pallas kernels: 72.8 us -> 70 us  [local(): pl.pallas_call(functools.partial(kernel, (ny, nx, nz, slots, per_col, sca...]
where the time goes in v3:
time: 73.2 us; the launch traced here: 72.5 us
  Pallas kernels  71.9 us (98%)
    pallas_call x1, Pallas kernels, local(): pl.pallas_call(functools.partial(kernel, (ny, nx, nz, slots, per_col, sca...  70 us
    pallas_call x1, Pallas kernels, local(): pl.pallas_call(finish, out_shape=tuple((jax.ShapeDtypeStruct(r.shape, r.d...  1.85 us

profile of v3, /device:TPU:6, one launch (start us, length us, event | category | flops | bytes accessed | tf_op | source)
XLA Modules:
  0.0 72.5 jit_solution(4961963478297977557)
XLA Ops:
  0.6 70.0 %shard_map.76 = (bf16[128,1536]{1,0:T(8,128)(2,1)}, bf16[128,256]{1,0:T(8,128)(2,1)}, f32[12,2048]{1,0:T(8,128)}) custom-call(bf16[128,256]{1,0:T(8,128)(2,1)} %x_hbm.1, bf16[12,8,128,128]{3,2,1,0:T(8,128)(2,1)} %w_hbm.1, bf16[128,1536]{1,0:T(8,128)(2,1)} %g_hbm.1, s32[8,112]{1,0:T(8,128)} %bitcast.2, s32[1,112]{1,0:T(1,128)} %bitcast.3), custom_call_target="tpu_custom_call" | custom-call | tf_op jit(solution)/shard_map/pallas_call | solution.py:437
  70.7 1.9 %shard_map.77 = (bf16[128,1536]{1,0:T(8,128)(2,1)}, bf16[128,256]{1,0:T(8,128)(2,1)}, f32[12,2048]{1,0:T(8,128)}) custom-call(bf16[128,1536]{1,0:T(8,128)(2,1)} %get-tuple-element.6.a_ref, bf16[128,256]{1,0:T(8,128)(2,1)} %get-tuple-element.7.b_ref, f32[12,2048]{1,0:T(8,128)} %get-tuple-element.8.c_ref), custom_call_target="tpu_custom_call" | custom-call | tf_op jit(solution)/shard_map/pallas_call | solution.py:483

commit v4 on v3

--- a/solution.py
+++ b/solution.py
@@ -59,8 +59,8 @@
     g_ref = gcat.at[0]
 
     barrier = pltpu.get_barrier_semaphore()
-    for o in range(1, owners):
-        pl.semaphore_signal(barrier, inc=1, device_id=dev(dp, peer_to(o)), device_id_type=MESH)
+    for v in NEAR:
+        pl.semaphore_signal(barrier, inc=1, device_id=dev(dp, shift(v)), device_id_type=MESH)
     for d in (along(0, 1), along(1, 1), along(0, 2), along(1, 2), dev(sibling, me)):
         pl.semaphore_signal(barrier, inc=1, device_id=d, device_id_type=MESH)
 
@@ -71,7 +71,7 @@
             for h in range(2):
                 lo = gi * 32 + h * 16
                 xt[2 * me + q, h, gi * 16:(gi + 1) * 16, :] = t[lo:lo + 16, :]
-    pl.semaphore_wait(barrier, owners - 1 + 5)
+    pl.semaphore_wait(barrier, len(NEAR) + 5)
 
     def plane_copy(tile, at, n, send, recv, move):
         here = pl.ds(2 * tile + at, n)

time: 73.2 us -> 72.4 us (0.989)
  no operation moved by 1% of the time
where the time goes in v4:
time: 72.4 us; the launch traced here: 72.3 us
  Pallas kernels  71.6 us (99%)
    pallas_call x1, Pallas kernels, local(): pl.pallas_call(functools.partial(kernel, (ny, nx, nz, slots, per_col, sca...  69.8 us
    pallas_call x1, Pallas kernels, local(): pl.pallas_call(finish, out_shape=tuple((jax.ShapeDtypeStruct(r.shape, r.d...  1.85 us

profile of v4, /device:TPU:6, one launch (start us, length us, event | category | flops | bytes accessed | tf_op | source)
XLA Modules:
  0.0 72.3 jit_solution(17260973276588953156)
XLA Ops:
  0.6 69.8 %shard_map.76 = (bf16[128,1536]{1,0:T(8,128)(2,1)}, bf16[128,256]{1,0:T(8,128)(2,1)}, f32[12,2048]{1,0:T(8,128)}) custom-call(bf16[128,256]{1,0:T(8,128)(2,1)} %x_hbm.1, bf16[12,8,128,128]{3,2,1,0:T(8,128)(2,1)} %w_hbm.1, bf16[128,1536]{1,0:T(8,128)(2,1)} %g_hbm.1, s32[8,112]{1,0:T(8,128)} %bitcast.2, s32[1,112]{1,0:T(1,128)} %bitcast.3), custom_call_target="tpu_custom_call" | custom-call | tf_op jit(solution)/shard_map/pallas_call | solution.py:437
  70.4 1.9 %shard_map.77 = (bf16[128,1536]{1,0:T(8,128)(2,1)}, bf16[128,256]{1,0:T(8,128)(2,1)}, f32[12,2048]{1,0:T(8,128)}) custom-call(bf16[128,1536]{1,0:T(8,128)(2,1)} %get-tuple-element.6.a_ref, bf16[128,256]{1,0:T(8,128)(2,1)} %get-tuple-element.7.b_ref, f32[12,2048]{1,0:T(8,128)} %get-tuple-element.8.c_ref), custom_call_target="tpu_custom_call" | custom-call | tf_op jit(solution)/shard_map/pallas_call | solution.py:483
